TPU v7x, 32 devices: a whole 2x2x4 slice. The times are simulated.
32 devices in a mesh: groups: 2 (over y), seq: 4 (over z), tensor: 4 (over x, core).
Axes of the slice: x: 2, y: 2, z: 4, core: 2. Of those that a mesh axis runs over, the one named last changes fastest.
Arguments:
- residual_in: float32 [1024, 4096], P(('groups', 'seq'), 'tensor'), parts along dimension 0, may hold values from -48 to 48
- norm_gain: float32 [4096], replicated, may hold values from 0.1 to 1.9
- in_weight: bfloat16 [3, 4096, 2048], P(None, 'seq', 'tensor'), may hold values from -0.09375 to 0.09375
- short_taps: float32 [3, 3, 2048], P(None, None, 'tensor'), may hold values from -3 to 3
- long_filter: float32 [2048, 512], P(('tensor', 'seq')), may hold values from -0.25 to 0.25
- out_weight: bfloat16 [4096, 2048], P('seq', 'tensor'), may hold values from -0.125 to 0.125
Outputs:
- block_out: float32 [1024, 4096], P(('groups', 'seq'), 'tensor'), parts along dimension 0
There are 2 independent parts, one for each index of `groups`. A program takes and returns all parts, laid end to end along the dimension named above; an argument that names none is the same for every part. Nothing has to cross between parts.
All inputs are finite; a program needn't handle non-finite values.
Results may differ from a plain program's by a relative error of at most 0.015.
Values may be sent and summed in bfloat16 or wider, within the bound.
A program may use at most 64 MiB of HBM per device.

v0:
```python
import math

import jax
import jax.numpy as jnp
from jax import lax
from jax.sharding import PartitionSpec as P

EPSILON = 1e-05


def shifted(value, axis, by):
    length = lax.axis_size(axis)
    pairs = [(i, i + by) for i in range(length) if 0 <= i + by < length]
    return lax.ppermute(value, axis, pairs)


def exact_product(form, left, right):
    return jnp.einsum(form, left, right, precision=lax.Precision.HIGHEST)


def angle_tables(modulus, count_a, count_b):
    index_a = jnp.arange(count_a, dtype=jnp.int32)[:, None]
    index_b = jnp.arange(count_b, dtype=jnp.int32)[None, :]
    theta = (index_a * index_b % modulus).astype(jnp.float32) * (2.0 * math.pi / modulus)
    return (jnp.cos(theta), jnp.sin(theta))


def split_length(full_length):
    low_factor = 1
    while full_length % (4 * low_factor) == 0 and 4 * low_factor * low_factor <= full_length:
        low_factor = low_factor * 2
    return (low_factor, full_length // low_factor)


def forward_spectrum(signal, low_factor, high_factor, all_tables):
    cos_high, sin_high, cos_twist, sin_twist, cos_low, sin_low = all_tables
    channel_count = signal.shape[0]
    blocks = signal.reshape(channel_count, high_factor // 2, low_factor)
    real_a = exact_product("cmp,mk->cpk", blocks, cos_high)
    imag_a = -exact_product("cmp,mk->cpk", blocks, sin_high)
    real_b = real_a * cos_twist + imag_a * sin_twist
    imag_b = imag_a * cos_twist - real_a * sin_twist
    real_x = exact_product("cpk,pj->cjk", real_b, cos_low) + exact_product(
        "cpk,pj->cjk", imag_b, sin_low
    )
    imag_x = exact_product("cpk,pj->cjk", imag_b, cos_low) - exact_product(
        "cpk,pj->cjk", real_b, sin_low
    )
    return (real_x, imag_x)


def inverse_signal(real_x, imag_x, low_factor, high_factor, all_tables):
    cos_high, sin_high, cos_twist, sin_twist, cos_low, sin_low = all_tables
    channel_count = real_x.shape[0]
    real_b = exact_product("cjk,pj->cpk", real_x, cos_low) - exact_product(
        "cjk,pj->cpk", imag_x, sin_low
    )
    imag_b = exact_product("cjk,pj->cpk", real_x, sin_low) + exact_product(
        "cjk,pj->cpk", imag_x, cos_low
    )
    real_c = real_b * cos_twist - imag_b * sin_twist
    imag_c = real_b * sin_twist + imag_b * cos_twist
    result = exact_product("cpk,mk->cmp", real_c, cos_high) - exact_product(
        "cpk,mk->cmp", imag_c, sin_high
    )
    full_length = low_factor * high_factor
    return (result / full_length).reshape(channel_count, full_length // 2)


def shards(residual_in, norm_gain, in_weight, short_taps, long_filter, out_weight):
    row_count, local_width = residual_in.shape
    full_rows = lax.all_gather(
        residual_in.astype(jnp.bfloat16), "tensor", axis=1, tiled=True
    ).astype(residual_in.dtype)
    mean_sq = jnp.mean(full_rows * full_rows, axis=1, keepdims=True)
    normed = (full_rows * lax.rsqrt(mean_sq + EPSILON) * norm_gain).astype(jnp.bfloat16)
    projected = jnp.einsum(
        "rd,sdc->scr",
        normed,
        lax.all_gather(in_weight, "seq", axis=1, tiled=True),
        preferred_element_type=jnp.float32,
    )
    reach = short_taps.shape[1] - 1
    earlier = shifted(projected[:, :, row_count - reach :], "seq", 1)
    extended = jnp.concatenate([earlier, projected], axis=2)
    mixed = short_taps[:, 0, :, None] * projected
    for offset in range(1, reach + 1):
        mixed = (
            mixed
            + short_taps[:, offset, :, None]
            * extended[:, :, reach - offset : reach - offset + row_count]
        )
    query = mixed[0]
    product_kv = mixed[1] * mixed[2]
    by_channel = lax.all_to_all(
        product_kv.astype(jnp.bfloat16), "seq", split_axis=0, concat_axis=1, tiled=True
    ).astype(product_kv.dtype)
    full_length = 2 * by_channel.shape[1]
    low_factor, high_factor = split_length(full_length)
    cos_high, sin_high = angle_tables(high_factor, high_factor // 2, high_factor)
    cos_twist, sin_twist = angle_tables(full_length, low_factor, high_factor)
    cos_low, sin_low = angle_tables(low_factor, low_factor, low_factor)
    all_tables = (cos_high, sin_high, cos_twist, sin_twist, cos_low, sin_low)
    signal_real, signal_imag = forward_spectrum(by_channel, low_factor, high_factor, all_tables)
    filter_real, filter_imag = forward_spectrum(long_filter, low_factor, high_factor, all_tables)
    conv = inverse_signal(
        signal_real * filter_real - signal_imag * filter_imag,
        signal_real * filter_imag + signal_imag * filter_real,
        low_factor,
        high_factor,
        all_tables,
    )
    returned = lax.all_to_all(
        conv.astype(jnp.bfloat16), "seq", split_axis=1, concat_axis=0, tiled=True
    ).astype(conv.dtype)
    gated = (query * returned).astype(jnp.bfloat16)
    terms = jnp.einsum(
        "cr,nc->rn",
        gated,
        lax.all_gather(out_weight, "seq", axis=0, tiled=True),
        preferred_element_type=jnp.float32,
    )
    summed = lax.psum_scatter(
        terms.astype(jnp.bfloat16), "tensor", scatter_dimension=1, tiled=True
    ).astype(jnp.float32)
    return residual_in + summed


def solution(mesh):
    return jax.shard_map(
        shards,
        mesh=mesh,
        in_specs=(
            P(("groups", "seq"), "tensor"),
            P(),
            P(None, "seq", "tensor"),
            P(None, None, "tensor"),
            P(("tensor", "seq"), None),
            P("seq", "tensor"),
        ),
        out_specs=P(("groups", "seq"), "tensor"),
        check_vma=False,
    )
```

profile of v0, /device:TPU:16, one launch (start us, length us, event | category | flops | bytes accessed | tf_op | source)
XLA Modules:
  0.0 369.3 jit_solution(11119482903067389308)
XLA Ops:
  6.5 1.8 convert_element_type.115
  8.3 0.0 all-gather.4.cloned.1.call-update
  8.4 0.0 all-gather.6.cloned.1.call-start
  8.4 0.7 all-gather.6.cloned.1.call-update
  9.1 0.0 all-gather.8.cloned.1.call-start
  9.2 0.7 all-gather.8.cloned.1.call-update
  9.9 0.0 copy-done.3
  9.9 16.8 %all-gather.4.cloned.1.call-done = bf16[128,4096]{1,0:T(8,128)(2,1)} async-done(((bf16[128,1024]{1,0:T(8,128)(2,1)}), bf16[128,4096]{1,0:T(8,128)(2,1)}) %all-gather.4.cloned.1.call-update) | async-done | bytes 1048592 | tf_op jit(solution)/shard_map/all_gather | solution.py:72
  26.7 1.5 fusion
  28.3 216.5 %all-gather.6.cloned.1.call-done = bf16[3,4096,512]{2,1,0:T(8,128)(2,1)} async-done(((bf16[3,1024,512]{2,1,0:T(8,128)(2,1)}), bf16[3,4096,512]{2,1,0:T(8,128)(2,1)}) %all-gather.6.cloned.1.call-update) | async-done | bytes 12582928 | tf_op jit(solution)/shard_map/all_gather | solution.py:80
  244.8 0.0 copy-done.2
  244.8 6.8 %convolution_bitcast_fusion = f32[3,512,128]{1,2,0:T(8,128)S(1)} fusion(bf16[3,4096,512]{2,1,0:T(8,128)(2,1)} %all-gather.6.cloned.1.call-done, bf16[128,4096]{1,0:T(8,128)(2,1)} %all-gather.4.cloned.1.call-done, f32[4096]{0:T(1024)S(1)} %copy-done.2, f32[128]{0:T(128)S(1)} %add_rsqrt_fusion), kind=kOutput, calls=%fused_computation.6 | convolution fusion | flops 1612709888 | bytes 14434816 | tf_op jit(solution)/shard_map/rd,sdc->scr/dot_general | solution.py:77
  251.6 2.1 collective-permute-start
  253.7 0.1 fusion.77
  253.8 0.1 copy.36
  253.9 0.1 copy.51
  254.0 0.1 copy.52
  254.1 5.4 %collective-permute-done = f32[3,512,2]{1,2,0:T(2,128)S(1)} collective-permute-done((f32[3,512,2]{1,2,0:T(2,128)S(1)}, f32[3,512,2]{1,2,0:T(2,128)S(1)}, u32[]{:S(2)}, u32[]{:S(2)}) %collective-permute-start) | collective-permute-done | bytes 12320 | tf_op jit(solution)/shard_map/ppermute | solution.py:14
  259.5 0.2 fusion.14
  259.8 0.7 copy.29
  260.5 4.2 %all-to-all-start = ((bf16[4,128,128]{1,2,0:T(8,128)(2,1)}), bf16[4,128,128]{1,2,0:T(8,128)(2,1)S(1)}, u32[]{:S(2)}, u32[]{:S(2)}) async-start(bf16[4,128,128]{1,2,0:T(8,128)(2,1)} %copy.29), calls=%async_computation | async-start | bytes 262144 | tf_op jit(solution)/shard_map/all_to_all | solution.py:95
  264.7 0.7 convolution_bitcast_fusion.1
  265.4 4.6 %all-to-all-done = bf16[4,128,128]{1,2,0:T(8,128)(2,1)S(1)} async-done(((bf16[4,128,128]{1,2,0:T(8,128)(2,1)}), bf16[4,128,128]{1,2,0:T(8,128)(2,1)S(1)}, u32[]{:S(2)}, u32[]{:S(2)}) %all-to-all-start) | async-done | bytes 131104 | tf_op jit(solution)/shard_map/all_to_all | solution.py:95
  270.0 0.5 convolution_negate_fusion.1
  270.5 0.5 fusion.43
  270.9 0.9 multiply_add_fusion.1
  271.8 0.9 fusion.25
  272.8 0.9 fusion.35
  273.7 0.9 fusion.29
  274.7 0.9 fusion.31
  275.6 0.9 convolution_subtract_fusion.1
  276.5 0.9 convolution_add_fusion.2
  277.5 0.9 convolution_add_fusion.1
  278.4 1.1 multiply_add_fusion
  279.5 0.7 fusion.18
  280.2 0.7 fusion.20
  280.8 0.7 convolution_add_fusion
  281.5 1.1 add_bitcast_fusion
  282.6 0.7 fusion.23
  283.3 0.7 fusion.6
  284.0 0.7 copy.55
  284.6 8.0 %all-to-all-start.1 = ((bf16[128,4,128]{0,2,1:T(8,128)(2,1)}), bf16[128,4,128]{0,2,1:T(8,128)(2,1)S(1)}, u32[]{:S(2)}, u32[]{:S(2)}) async-start(bf16[128,4,128]{0,2,1:T(8,128)(2,1)} %bitcast.26), calls=%async_computation.1 | async-start | bytes 262144 | tf_op jit(solution)/shard_map/all_to_all | solution.py:113
  292.7 37.1 %all-gather.8.cloned.1.call-done = bf16[4096,512]{1,0:T(8,128)(2,1)} async-done(((bf16[1024,512]{1,0:T(8,128)(2,1)}), bf16[4096,512]{1,0:T(8,128)(2,1)}) %all-gather.8.cloned.1.call-update) | async-done | bytes 4194320 | tf_op jit(solution)/shard_map/all_gather | solution.py:120
  329.8 0.0 all-to-all-done.1
  329.8 4.7 %convolution_convert_fusion = bf16[128,4096]{1,0:T(8,128)(2,1)} fusion(bf16[4096,512]{1,0:T(8,128)(2,1)} %all-gather.8.cloned.1.call-done, f32[3,512,128]{1,2,0:T(8,128)S(1)} %fusion.14, bf16[128,4,128]{0,2,1:T(8,128)(2,1)S(1)} %all-to-all-done.1), kind=kOutput, calls=%fused_computation | convolution fusion | flops 537591808 | bytes 5636096 | tf_op jit(solution)/shard_map/cr,nc->rn/dot_general | solution.py:117
  334.4 0.0 reduce-scatter.2.cloned.1.call-update
  334.4 26.5 %reduce-scatter.2.cloned.1.call-done = bf16[128,1024]{1,0:T(8,128)(2,1)} async-done(((bf16[128,4096]{1,0:T(8,128)(2,1)}), bf16[128,1024]{1,0:T(8,128)(2,1)}) %reduce-scatter.2.cloned.1.call-update) | async-done | bytes 262160 | tf_op jit(solution)/shard_map/reduce_scatter | solution.py:123
  361.0 1.8 convert_add_fusion
  (15 shorter events, 0.1 us)
Async XLA Ops:
  6.5 3.3 copy-start.3
  6.5 238.3 %copy-start.2 = (f32[4096]{0:T(1024)S(1)}, f32[4096]{0:T(1024)}, u32[]{:S(2)}) copy-start(f32[4096]{0:T(1024)} %param.7) | copy-start | bytes 49156
  6.5 20.2 %all-gather.4.cloned.1.call-start = ((), (), s32[]{:S(2)}) async-start(), calls=%async_computation.3 | async-start | bytes 1310720 | tf_op jit(solution)/shard_map/all_gather | solution.py:72
  8.4 236.4 %all-gather.6.cloned.1.call-start = ((), (), s32[]{:S(2)}) async-start(), calls=%async_computation.4 | async-start | bytes 15728640 | tf_op jit(solution)/shard_map/all_gather | solution.py:80
  9.1 320.6 %all-gather.8.cloned.1.call-start = ((), (), s32[]{:S(2)}) async-start(), calls=%async_computation.5 | async-start | bytes 5242880 | tf_op jit(solution)/shard_map/all_gather | solution.py:120
  28.3 225.5 %copy-start.1 = (f32[128,512]{1,0:T(8,128)S(1)}, f32[128,512]{1,0:T(8,128)}, u32[]{:S(2)}) copy-start(f32[128,512]{1,0:T(8,128)} %param.10) | copy-start | bytes 786436
  251.6 7.9 %collective-permute-start = (f32[3,512,2]{1,2,0:T(2,128)S(1)}, f32[3,512,2]{1,2,0:T(2,128)S(1)}, u32[]{:S(2)}, u32[]{:S(2)}) collective-permute-start(f32[3,512,2]{1,2,0:T(2,128)S(1)} %slice.36), channel_id=1, source_target_pairs={{0,4},{4,8},{8,12},{1,5},{5,9},{9,13},{2,6},{6,10},{10,14},{3,7},{... | collective-permute-start | bytes 36872 | tf_op jit(solution)/shard_map/ppermute | solution.py:14
  260.5 9.5 %all-to-all-start = ((bf16[4,128,128]{1,2,0:T(8,128)(2,1)}), bf16[4,128,128]{1,2,0:T(8,128)(2,1)S(1)}, u32[]{:S(2)}, u32[]{:S(2)}) async-start(bf16[4,128,128]{1,2,0:T(8,128)(2,1)} %copy.29), calls=%async_computation | async-start | bytes 262144 | tf_op jit(solution)/shard_map/all_to_all | solution.py:95
  284.6 45.1 %all-to-all-start.1 = ((bf16[128,4,128]{0,2,1:T(8,128)(2,1)}), bf16[128,4,128]{0,2,1:T(8,128)(2,1)S(1)}, u32[]{:S(2)}, u32[]{:S(2)}) async-start(bf16[128,4,128]{0,2,1:T(8,128)(2,1)} %bitcast.26), calls=%async_computation.1 | async-start | bytes 262144 | tf_op jit(solution)/shard_map/all_to_all | solution.py:113
  292.7 68.3 %copy-start = (f32[128,1024]{1,0:T(8,128)S(1)}, f32[128,1024]{1,0:T(8,128)}, u32[]{:S(2)}) copy-start(f32[128,1024]{1,0:T(8,128)} %param.6) | copy-start | bytes 1572868
  292.7 68.3 %reduce-scatter.2.cloned.1.call-start = ((), (), s32[]{:S(2)}) async-start(), calls=%async_computation.6 | async-start | bytes 1310720 | tf_op jit(solution)/shard_map/reduce_scatter | solution.py:123
Sparse Core Ops, SparseCore 0:
  8.9 17.7 all-gather.3
  28.3 216.4 all-gather.5
  246.4 83.3 all-gather.7
  334.6 26.3 reduce-scatter.1
where the time goes:
time: 371 us; the launch traced here: 369 us
  waiting for transfers between devices  308 us (83%)
  matrix products  26 us (7%)
  starting transfers between devices  14.4 us (4%)
  between operations  13.4 us (4%)
  other arithmetic  5.49 us (1%)
    all_gather x1, waiting for transfers between devices, shards(): lax.all_gather(in_weight, 'seq', axis=1, tiled=True)  217 us
    all_gather x1, waiting for transfers between devices, shards(): lax.all_gather(out_weight, 'seq', axis=0, tiled=True)  37.1 us
    reduce_scatter x1, waiting for transfers between devices, shards(): lax.psum_scatter(terms.astype(jnp.bfloat16), 'tensor', scatter_dimension=...  26.5 us
    all_gather x1, waiting for transfers between devices, shards(): lax.all_gather(residual_in.astype(jnp.bfloat16), 'tensor', axis=1, tiled=...  16.8 us
    dot_general x18, matrix products, exact_product(): return jnp.einsum(form, left, right, precision=lax.Precision.HIGHEST)  14.6 us
    all_to_all x1, starting transfers between devices, shards(): lax.all_to_all(conv.astype(jnp.bfloat16), 'seq', split_axis=1, concat_axi...  8.02 us
  transfers between devices with their start and end apart: 7, of which 6 were waited for; matrix products, arithmetic and copies ran while one was open for 7% of the time, Pallas kernels for 0%

commit v1 on v0

--- a/solution.py
+++ b/solution.py
@@ -2,7 +2,11 @@
 
 import jax
 import jax.numpy as jnp
+import ml_dtypes
+import numpy as np
 from jax import lax
+from jax.experimental import pallas as pl
+from jax.experimental.pallas import tpu as pltpu
 from jax.sharding import PartitionSpec as P
 
 EPSILON = 1e-05
@@ -126,9 +130,379 @@
     return residual_in + summed
 
 
+MESH = pl.DeviceIdType.MESH
+
+
+def transform_tables(length):
+    index = np.arange(length)
+    turns = ((2 * index[:, None] + 1) * index[None, :]) % (4 * length)
+    theta = turns.astype(np.float64) * (math.pi / (2 * length))
+    table = np.concatenate([np.cos(theta), np.sin(theta)], axis=0).astype(np.float32)
+    high = table.astype(ml_dtypes.bfloat16)
+    low = (table - high.astype(np.float32)).astype(ml_dtypes.bfloat16)
+    return (high, low, np.ascontiguousarray(high.T), np.ascontiguousarray(low.T))
+
+
+def two_parts(value):
+    high = value.astype(jnp.bfloat16)
+    low = (value - high.astype(jnp.float32)).astype(jnp.bfloat16)
+    return (high, low)
+
+
+def matmul(left, right):
+    return jnp.dot(left, right, preferred_element_type=jnp.float32)
+
+
+def matmul_nt(left, right):
+    return lax.dot_general(left, right, (((1,), (1,)), ((), ())), preferred_element_type=jnp.float32)
+
+
+def block_kernel(
+    x_ref, gain_ref, w_hbm, taps_ref, filter_ref, wo_hbm, ah_hbm, al_hbm, bh_hbm, bl_hbm,
+    out_ref,
+    wv, wo, ah, al, bh, bl, xb, xg, part, sendb, from_low, from_high, squares, spectrum,
+    gathered, terms, sibling_in, cross_in, final_in,
+    load_sem, x_send, x_recv, p_send, low_recv, high_recv, q_send, q_recv,
+    g_right, g_left, g_recv, t_send, t_recv,
+):
+    s = lax.axis_index("seq")
+    t = lax.axis_index("tensor")
+    n = 4
+    rows, width = x_ref.shape
+    ch = filter_ref.shape[0]
+    length = filter_ref.shape[1]
+    sib = t + 1 - 2 * lax.rem(t, 2)
+    far = lax.rem(t + 2, n)
+    far_sib = lax.rem(sib + 2, n)
+
+    loads = []
+    for d in range(n):
+        for j in range(3):
+            loads.append(pltpu.make_async_copy(
+                w_hbm.at[j, :, pl.ds(d * ch, ch)],
+                wv.at[d, :, pl.ds(j * ch, ch)],
+                load_sem.at[d * 3 + j],
+            ))
+    for i, (source, target) in enumerate(
+        ((ah_hbm, ah), (al_hbm, al), (wo_hbm, wo), (bh_hbm, bh), (bl_hbm, bl))
+    ):
+        loads.append(pltpu.make_async_copy(source, target, load_sem.at[3 * n + i]))
+    for load in loads:
+        load.start()
+
+    barrier = pltpu.get_barrier_semaphore()
+    for k in range(1, n):
+        pl.semaphore_signal(barrier, inc=1, device_id={"seq": lax.rem(s + k, n), "tensor": t}, device_id_type=MESH)
+        pl.semaphore_signal(barrier, inc=1, device_id={"seq": s, "tensor": lax.rem(t + k, n)}, device_id_type=MESH)
+
+    @pl.when(s != t)
+    def _():
+        pl.semaphore_signal(barrier, inc=1, device_id={"seq": t, "tensor": s}, device_id_type=MESH)
+
+    xb[...] = x_ref[...].astype(jnp.bfloat16)
+
+    @pl.when(s != t)
+    def _():
+        pl.semaphore_wait(barrier, 2 * n - 1)
+
+    @pl.when(s == t)
+    def _():
+        pl.semaphore_wait(barrier, 2 * n - 2)
+
+    def remote(source, target, send, recv, to_s, to_t):
+        return pltpu.make_async_remote_copy(
+            src_ref=source, dst_ref=target, send_sem=send, recv_sem=recv,
+            device_id={"seq": to_s, "tensor": to_t}, device_id_type=MESH,
+        )
+
+    swap = remote(xb, xg.at[s], x_send.at[0], x_recv.at[s], t, s)
+    swapped = remote(xb, xg.at[t], x_send.at[0], x_recv.at[t], t, s)
+
+    @pl.when(s != t)
+    def _():
+        swap.start()
+
+    fh, fl = two_parts(filter_ref[...])
+    loads[3 * n].wait()
+    loads[3 * n + 1].wait()
+    spectrum[...] = matmul_nt(ah[...], fh) + matmul_nt(ah[...], fl) + matmul_nt(al[...], fh)
+
+    for load in loads[: 3 * n]:
+        load.wait()
+
+    @pl.when(s != t)
+    def _():
+        swapped.wait_recv()
+
+    @pl.when(s == t)
+    def _():
+        xg[t] = xb[...]
+
+    def slot_copy(slot, send, to_t):
+        return remote(xg.at[slot], xg.at[slot], send, x_recv.at[slot], s, to_t)
+
+    to_far = slot_copy(t, x_send.at[1], far)
+    to_sib = slot_copy(t, x_send.at[2], sib)
+    relay = slot_copy(far, x_send.at[3], sib)
+    to_far.start()
+    to_sib.start()
+
+    gain = gain_ref[:, pl.ds(pl.multiple_of(s * width, 128), width)]
+    ones = jnp.ones((8, width), jnp.bfloat16)
+
+    def p_copy(p, d, up):
+        target, recv = (from_low, low_recv) if up else (from_high, high_recv)
+        return remote(
+            sendb.at[p, d], target.at[p, d], p_send.at[p, d], recv.at[p, d],
+            s + 1 if up else s - 1, t,
+        )
+
+    def dots(p):
+        features = xg[p].astype(jnp.float32)
+        sh, sl = two_parts(features * features)
+        squares[s, :, pl.ds(pl.multiple_of(p * rows, 128), rows)] = matmul_nt(ones, sh) + matmul_nt(ones, sl)
+        y = (features * gain).astype(jnp.bfloat16)
+
+        @pl.loop(0, n)
+        def _(d):
+            part[p, d] = matmul(y, wv[d])
+
+        @pl.when(s == 0)
+        def _():
+            @pl.loop(0, n - 1)
+            def _(i):
+                d = n - 1 - i
+                sendb[p, d] = part[p, d].astype(jnp.bfloat16)
+                p_copy(p, d, True).start()
+
+        @pl.when(s == n - 1)
+        def _():
+            @pl.loop(0, n - 1)
+            def _(d):
+                sendb[p, d] = part[p, d].astype(jnp.bfloat16)
+                p_copy(p, d, False).start()
+
+    def chain(p):
+        @pl.when((s > 0) & (s < n - 1))
+        def _():
+            @pl.loop(0, n - 1)
+            def _(i):
+                d = n - 1 - i
+
+                @pl.when(d > s)
+                def _():
+                    p_copy(p, d, True).wait_recv()
+                    sendb[p, d] = (part[p, d] + from_low[p, d].astype(jnp.float32)).astype(jnp.bfloat16)
+                    p_copy(p, d, True).start()
+
+                @pl.when(i < s)
+                def _():
+                    p_copy(p, i, False).wait_recv()
+                    sendb[p, i] = (part[p, i] + from_high[p, i].astype(jnp.float32)).astype(jnp.bfloat16)
+                    p_copy(p, i, False).start()
+
+    dots(t)
+    slot_copy(sib, x_send.at[2], sib).wait_recv()
+    dots(sib)
+    slot_copy(far, x_send.at[1], far).wait_recv()
+    relay.start()
+    dots(far)
+    chain(t)
+    slot_copy(far_sib, x_send.at[3], sib).wait_recv()
+    dots(far_sib)
+
+    q_copies = []
+    for k in range(1, n):
+        q_copy = remote(squares.at[s], squares.at[s], q_send.at[k], q_recv.at[s], lax.rem(s + k, n), t)
+        q_copy.start()
+        q_copies.append(q_copy)
+    chain(sib)
+    chain(far)
+    chain(far_sib)
+
+    for k in range(1, n):
+        other = lax.rem(s + k, n)
+        remote(squares.at[other], squares.at[other], q_send.at[k], q_recv.at[other], other, t).wait_recv()
+    total = squares[0] + squares[1] + squares[2] + squares[3]
+    scale = lax.rsqrt(total * (1.0 / (n * width)) + EPSILON)
+    scale = jnp.transpose(jnp.broadcast_to(scale[0:1], (ch, length)))
+
+    for p in (t, sib, far, far_sib):
+        @pl.when(s > 0)
+        def _():
+            p_copy(p, s, True).wait_recv()
+            part[p, s] += from_low[p, s].astype(jnp.float32)
+
+        @pl.when(s < n - 1)
+        def _():
+            p_copy(p, s, False).wait_recv()
+            part[p, s] += from_high[p, s].astype(jnp.float32)
+
+    row = lax.broadcasted_iota(jnp.int32, (length, ch), 0)
+    mixed = []
+    for j in range(3):
+        projected = jnp.concatenate([part[p, s, :, j * ch:(j + 1) * ch] for p in range(n)], axis=0) * scale
+        taps = [taps_ref[j, o:o + 1, pl.ds(pl.multiple_of(s * ch, 128), ch)] for o in range(3)]
+        value = taps[0] * projected
+        for o in range(1, 3):
+            value = value + taps[o] * jnp.where(row >= o, pltpu.roll(projected, o, 0), 0.0)
+        mixed.append(value)
+    query = mixed[0]
+    kh, kl = two_parts(mixed[1] * mixed[2])
+    both = matmul(ah[...], jnp.concatenate([kh, kl], axis=1))
+    signal = both[:, :ch] + both[:, ch:] + matmul(al[...], kh)
+    a, b = signal[:length], signal[length:]
+    c, e = spectrum[:length], spectrum[length:]
+    yh, yl = two_parts(jnp.concatenate([a * c - b * e, a * e + b * c], axis=0))
+    for load in loads[3 * n + 2:]:
+        load.wait()
+    both = matmul(bh[...], jnp.concatenate([yh, yl], axis=1))
+    conv = (both[:, :ch] + both[:, ch:] + matmul(bl[...], yh)) * (1.0 / length)
+
+    def lanes(i):
+        return pl.ds(pl.multiple_of(i * ch, 128), ch)
+
+    gathered[:, lanes(s)] = (query * conv).astype(jnp.bfloat16)
+
+    def g_copy(i, up):
+        sems = g_right if up else g_left
+        return remote(
+            gathered.at[:, lanes(i)], gathered.at[:, lanes(i)], sems.at[i], g_recv.at[i],
+            s + 1 if up else s - 1, t,
+        )
+
+    @pl.when(s < n - 1)
+    def _():
+        g_copy(s, True).start()
+
+    @pl.when(s > 0)
+    def _():
+        g_copy(s, False).start()
+
+    for k in range(1, n):
+        @pl.when(s - k >= 0)
+        def _():
+            g_copy(s - k, True).wait_recv()
+
+            @pl.when(s < n - 1)
+            def _():
+                g_copy(s - k, True).start()
+
+        @pl.when(s + k < n)
+        def _():
+            g_copy(s + k, False).wait_recv()
+
+            @pl.when(s > 0)
+            def _():
+                g_copy(s + k, False).start()
+
+    def term(p):
+        return matmul_nt(gathered[pl.ds(pl.multiple_of(p * rows, 128), rows), :], wo[...])
+
+    far_out = remote(terms.at[0], sibling_in.at[0], t_send.at[0], t_recv.at[0], s, sib)
+    own_out = remote(terms.at[1], sibling_in.at[1], t_send.at[1], t_recv.at[1], s, sib)
+    cross = remote(terms.at[2], cross_in, t_send.at[2], t_recv.at[2], s, far)
+    final = remote(terms.at[3], final_in, t_send.at[3], t_recv.at[3], t, s)
+    terms[0] = term(far_sib).astype(jnp.bfloat16)
+    far_out.start()
+    terms[1] = term(sib).astype(jnp.bfloat16)
+    own_out.start()
+    far_term = term(far)
+    far_out.wait_recv()
+    terms[2] = (far_term + sibling_in[0].astype(jnp.float32)).astype(jnp.bfloat16)
+    cross.start()
+    own_term = term(t)
+    own_out.wait_recv()
+    own_term = own_term + sibling_in[1].astype(jnp.float32)
+    cross.wait_recv()
+    own_term = own_term + cross_in[...].astype(jnp.float32)
+
+    @pl.when(s != t)
+    def _():
+        terms[3] = own_term.astype(jnp.bfloat16)
+        final.start()
+        final.wait_recv()
+        out_ref[...] = x_ref[...] + final_in[...].astype(jnp.float32)
+
+    @pl.when(s == t)
+    def _():
+        out_ref[...] = x_ref[...] + own_term
+
+    @pl.when(s != t)
+    def _():
+        swap.wait_send()
+        final.wait_send()
+
+    for copy in [to_far, to_sib, relay, far_out, own_out, cross] + q_copies:
+        copy.wait_send()
+    for p in (t, sib, far, far_sib):
+        @pl.loop(0, n)
+        def _(d):
+            @pl.when(d > s)
+            def _():
+                p_copy(p, d, True).wait_send()
+
+            @pl.when(d < s)
+            def _():
+                p_copy(p, d, False).wait_send()
+
+    @pl.loop(0, n)
+    def _(i):
+        @pl.when((i <= s) & (s < n - 1))
+        def _():
+            g_copy(i, True).wait_send()
+
+        @pl.when((i >= s) & (s > 0))
+        def _():
+            g_copy(i, False).wait_send()
+
+
+def kernel_shards(residual_in, norm_gain, in_weight, short_taps, long_filter, out_weight):
+    n = 4
+    rows, width = residual_in.shape
+    ch, length = long_filter.shape
+    tables = [jnp.asarray(table) for table in transform_tables(length)]
+    vmem, hbm = pl.BlockSpec(memory_space=pltpu.VMEM), pl.BlockSpec(memory_space=pl.ANY)
+    dma = pltpu.SemaphoreType.DMA
+    bf16, f32 = jnp.bfloat16, jnp.float32
+    return pl.pallas_call(
+        block_kernel,
+        out_shape=jax.ShapeDtypeStruct((rows, width), f32),
+        in_specs=[vmem, vmem, hbm, vmem, vmem] + [hbm] * 5,
+        out_specs=vmem,
+        scratch_shapes=[
+            pltpu.VMEM((n, width, 3 * ch), bf16),
+            pltpu.VMEM(out_weight.shape, bf16),
+            pltpu.VMEM((2 * length, length), bf16),
+            pltpu.VMEM((2 * length, length), bf16),
+            pltpu.VMEM((length, 2 * length), bf16),
+            pltpu.VMEM((length, 2 * length), bf16),
+            pltpu.VMEM((rows, width), bf16),
+            pltpu.VMEM((n, rows, width), bf16),
+            pltpu.VMEM((n, n, rows, 3 * ch), f32),
+            pltpu.VMEM((n, n, rows, 3 * ch), bf16),
+            pltpu.VMEM((n, n, rows, 3 * ch), bf16),
+            pltpu.VMEM((n, n, rows, 3 * ch), bf16),
+            pltpu.VMEM((n, 8, length), f32),
+            pltpu.VMEM((2 * length, ch), f32),
+            pltpu.VMEM((length, n * ch), bf16),
+            pltpu.VMEM((n, rows, width), bf16),
+            pltpu.VMEM((2, rows, width), bf16),
+            pltpu.VMEM((rows, width), bf16),
+            pltpu.VMEM((rows, width), bf16),
+            dma((3 * n + 5,)), dma((n,)), dma((n,)), dma((n, n)), dma((n, n)), dma((n, n)),
+            dma((n,)), dma((n,)), dma((n,)), dma((n,)), dma((n,)), dma((n,)), dma((n,)),
+        ],
+        compiler_params=pltpu.CompilerParams(
+            collective_id=0, has_side_effects=True, vmem_limit_bytes=48 * 1024 * 1024
+        ),
+    )(residual_in, norm_gain[None], in_weight, short_taps, long_filter, out_weight, *tables)
+
+
 def solution(mesh):
+    square = mesh.shape["seq"] == 4 and mesh.shape["tensor"] == 4
     return jax.shard_map(
-        shards,
+        kernel_shards if square else shards,
         mesh=mesh,
         in_specs=(
             P(("groups", "seq"), "tensor"),

time: 371 us -> 109 us (0.29)
  waiting for transfers between devices: 308 us -> 0 us
  Pallas kernels: 0 us -> 99.8 us
  matrix products: 26 us -> 0 us
  starting transfers between devices: 14.4 us -> 0 us
  between operations: 13.4 us -> 0.02 us
  local copies, waits for them, and re-layouts: 1.71 us -> 9.14 us
  other arithmetic: 5.49 us -> 0 us
    all_gather x3 -> x0, waiting for transfers between devices: 270 us -> none  [the longest x1 217 us: shards(): lax.all_gather(in_weight, 'seq', axis=1, tiled=True)]
    pallas_call x0 -> x1, Pallas kernels: none -> 99.8 us  [kernel_shards(): pl.pallas_call(block_kernel, out_shape=jax.ShapeDtypeStruct((rows, width)...]
    reduce_scatter x1 -> x0, waiting for transfers between devices: 26.5 us -> none  [shards(): lax.psum_scatter(terms.astype(jnp.bfloat16), 'tensor', scatter_dimension=...]
    dot_general x20 -> x0, matrix products: 26 us -> none  [the longest x18 14.6 us: exact_product(): return jnp.einsum(form, left, right, precision=lax.Precision.HIGHEST)]
    all_to_all x2 -> x0, starting transfers between devices: 12.2 us -> none  [the longest x1 8.02 us: shards(): lax.all_to_all(conv.astype(jnp.bfloat16), 'seq', split_axis=1, concat_axi...]
    unnamed x11 -> x17, local copies, waits for them, and re-layouts: 0.15 us -> 9.14 us
    ppermute x1 -> x0, waiting for transfers between devices: 5.44 us -> none  [shifted(): return lax.ppermute(value, axis, pairs)]
    all_to_all x2 -> x0, waiting for transfers between devices: 4.57 us -> none  [the longest x1 4.56 us: shards(): lax.all_to_all(product_kv.astype(jnp.bfloat16), 'seq', split_axis=0, conc...]
  transfers between devices with their start and end apart: 7 -> 0, of which waited for: 6 -> 0; matrix products, arithmetic and copies ran while one was open for 7% -> 0% of each run, Pallas kernels for 0% -> 0%
where the time goes in v1:
time: 109 us
  Pallas kernels  99.8 us (92%)
  local copies, waits for them, and re-layouts  9.14 us (8%)
    pallas_call x1, Pallas kernels, kernel_shards(): pl.pallas_call(block_kernel, out_shape=jax.ShapeDtypeStruct((rows, width)...  99.8 us
    unnamed x17, local copies, waits for them, and re-layouts  9.14 us

profile of v1, /device:TPU:16, one launch (start us, length us, event | category | flops | bytes accessed | tf_op | source)
XLA Modules:
  0.0 108.9 jit_solution(6024846749998510019)
XLA Ops:
  0.0 0.0 copy-start
  0.0 1.2 %copy-done = bf16[1024,512]{1,0:T(8,128)(2,1)S(1)} copy-done((bf16[1024,512]{1,0:T(8,128)(2,1)S(1)}, bf16[1024,512]{1,0:T(8,128)(2,1)}, u32[]{:S(2)}) %copy-start) | copy-done | bytes 1048600
  1.2 0.0 copy-start.1
  1.2 1.2 %copy-done.1 = bf16[512,1024]{1,0:T(8,128)(2,1)S(1)} copy-done((bf16[512,1024]{1,0:T(8,128)(2,1)S(1)}, bf16[512,1024]{1,0:T(8,128)(2,1)}, u32[]{:S(2)}) %copy-start.1) | copy-done | bytes 1048600
  2.5 0.0 copy-start.2
  2.5 1.2 %copy-done.2 = bf16[1024,512]{1,0:T(8,128)(2,1)S(1)} copy-done((bf16[1024,512]{1,0:T(8,128)(2,1)S(1)}, bf16[1024,512]{1,0:T(8,128)(2,1)}, u32[]{:S(2)}) %copy-start.2) | copy-done | bytes 1048600
  3.7 0.0 copy-start.3
  3.7 1.2 %copy-done.3 = bf16[1024,512]{1,0:T(8,128)(2,1)S(1)} copy-done((bf16[1024,512]{1,0:T(8,128)(2,1)S(1)}, bf16[1024,512]{1,0:T(8,128)(2,1)}, u32[]{:S(2)}) %copy-start.3) | copy-done | bytes 1048600
  4.9 0.0 copy-start.4
  4.9 1.0 copy-done.4
  5.9 0.0 copy-start.5
  5.9 0.9 copy-done.5
  6.9 0.0 copy-start.6
  6.9 0.7 copy-done.6
  7.6 0.0 copy-start.7
  7.6 0.7 copy-done.7
  8.3 99.8 %shard_map.100 = f32[128,1024]{1,0:T(8,128)S(1)} custom-call(f32[128,1024]{1,0:T(8,128)S(1)} %copy-done.4, f32[1,4096]{1,0:T(1,128)S(1)} %bitcast.1, bf16[3,1024,512]{2,1,0:T(8,128)(2,1)} %w_hbm.1, f32[3,3,512]{2,1,0:T(4,128)S(1)} %copy-done.6, f32[128,512]{1,0:T(8,128)S(1)} %copy-done.5, bf16[1024,512]{1,0:T(8,128)(2,1)S(1)} %copy-done, ...), custom_call_target="tpu_custom_call" | custom-call | tf_op jit(solution)/shard_map/pallas_call | solution.py:468
  108.1 0.8 copy.12
Async XLA Ops:
  0.0 1.2 %copy-start = (bf16[1024,512]{1,0:T(8,128)(2,1)S(1)}, bf16[1024,512]{1,0:T(8,128)(2,1)}, u32[]{:S(2)}) copy-start(bf16[1024,512]{1,0:T(8,128)(2,1)} %wo_hbm.1) | copy-start | bytes 3145732
  1.2 1.2 %copy-start.1 = (bf16[512,1024]{1,0:T(8,128)(2,1)S(1)}, bf16[512,1024]{1,0:T(8,128)(2,1)}, u32[]{:S(2)}) copy-start(bf16[512,1024]{1,0:T(8,128)(2,1)} %constant.10.clone.bh_hbm) | copy-start | bytes 3145732
  2.5 1.2 %copy-start.2 = (bf16[1024,512]{1,0:T(8,128)(2,1)S(1)}, bf16[1024,512]{1,0:T(8,128)(2,1)}, u32[]{:S(2)}) copy-start(bf16[1024,512]{1,0:T(8,128)(2,1)} %constant.9.clone.al_hbm) | copy-start | bytes 3145732
  3.7 1.2 %copy-start.3 = (bf16[1024,512]{1,0:T(8,128)(2,1)S(1)}, bf16[1024,512]{1,0:T(8,128)(2,1)}, u32[]{:S(2)}) copy-start(bf16[1024,512]{1,0:T(8,128)(2,1)} %constant.8.clone.ah_hbm) | copy-start | bytes 3145732
  4.9 1.0 copy-start.4
  5.9 0.9 copy-start.5
  6.9 0.7 copy-start.6
  7.6 0.7 copy-start.7

commit v2 on v1

--- a/solution.py
+++ b/solution.py
@@ -158,10 +158,10 @@
 
 
 def block_kernel(
-    x_ref, gain_ref, w_hbm, taps_ref, filter_ref, wo_hbm, ah_hbm, al_hbm, bh_hbm, bl_hbm,
+    x_hbm, gain_hbm, w_hbm, taps_hbm, filter_hbm, wo_hbm, ah_hbm, al_hbm, bh_hbm, bl_hbm,
     out_ref,
-    wv, wo, ah, al, bh, bl, xb, xg, part, sendb, from_low, from_high, squares, spectrum,
-    gathered, terms, sibling_in, cross_in, final_in,
+    x_ref, gain_ref, taps_ref, filter_ref, wv, wo, ah, al, bh, bl, xb, xg, part, sendb, from_low, from_high, squares, spectrum,
+    gathered, terms, terms_acc, sibling_in, cross_in, final_in,
     load_sem, x_send, x_recv, p_send, low_recv, high_recv, q_send, q_recv,
     g_right, g_left, g_recv, t_send, t_recv,
 ):
@@ -175,20 +175,28 @@
     far = lax.rem(t + 2, n)
     far_sib = lax.rem(sib + 2, n)
 
+    chunks = 4
+    step = rows // chunks
+
+    def lanes(i):
+        return pl.ds(pl.multiple_of(i * ch, 128), ch)
+
     loads = []
     for d in range(n):
         for j in range(3):
             loads.append(pltpu.make_async_copy(
-                w_hbm.at[j, :, pl.ds(d * ch, ch)],
+                w_hbm.at[(j + 1) % 3, :, pl.ds(d * ch, ch)],
                 wv.at[d, :, pl.ds(j * ch, ch)],
                 load_sem.at[d * 3 + j],
             ))
-    for i, (source, target) in enumerate(
-        ((ah_hbm, ah), (al_hbm, al), (wo_hbm, wo), (bh_hbm, bh), (bl_hbm, bl))
-    ):
+    for i, (source, target) in enumerate((
+        (ah_hbm, ah), (al_hbm, al), (wo_hbm, wo), (bh_hbm, bh), (bl_hbm, bl),
+        (x_hbm, x_ref), (filter_hbm, filter_ref), (taps_hbm.at[:, :, lanes(s)], taps_ref),
+        (gain_hbm.at[:, pl.ds(pl.multiple_of(s * width, 128), width)], gain_ref),
+    )):
         loads.append(pltpu.make_async_copy(source, target, load_sem.at[3 * n + i]))
-    for load in loads:
-        load.start()
+    x_load, filter_load, taps_load, gain_load = loads[3 * n + 5:]
+    x_load.start()
 
     barrier = pltpu.get_barrier_semaphore()
     for k in range(1, n):
@@ -199,6 +207,10 @@
     def _():
         pl.semaphore_signal(barrier, inc=1, device_id={"seq": t, "tensor": s}, device_id_type=MESH)
 
+    filter_load.start()
+    for load in loads[3 * n:3 * n + 2] + loads[:3 * n] + [gain_load, taps_load] + loads[3 * n + 2:3 * n + 5]:
+        load.start()
+    x_load.wait()
     xb[...] = x_ref[...].astype(jnp.bfloat16)
 
     @pl.when(s != t)
@@ -215,47 +227,72 @@
             device_id={"seq": to_s, "tensor": to_t}, device_id_type=MESH,
         )
 
-    swap = remote(xb, xg.at[s], x_send.at[0], x_recv.at[s], t, s)
-    swapped = remote(xb, xg.at[t], x_send.at[0], x_recv.at[t], t, s)
+    def piece(h):
+        return pl.ds(h * step, step)
+
+    def swap(h, slot):
+        return remote(
+            xb.at[piece(h)], xg.at[slot, piece(h)], x_send.at[0, h], x_recv.at[slot, h], t, s
+        )
 
     @pl.when(s != t)
     def _():
-        swap.start()
-
+        for h in range(chunks):
+            swap(h, s).start()
+
+    filter_load.wait()
     fh, fl = two_parts(filter_ref[...])
     loads[3 * n].wait()
     loads[3 * n + 1].wait()
     spectrum[...] = matmul_nt(ah[...], fh) + matmul_nt(ah[...], fl) + matmul_nt(al[...], fh)
 
+    def slot_copy(slot, which, to_t, h):
+        return remote(
+            xg.at[slot, piece(h)], xg.at[slot, piece(h)], x_send.at[which, h], x_recv.at[slot, h], s, to_t
+        )
+
+    @pl.when(s == t)
+    def _():
+        xg[t] = xb[...]
+
+    for h in range(chunks):
+        @pl.when(s != t)
+        def _():
+            swap(h, t).wait_recv()
+
+        slot_copy(t, 1, far, h).start()
+        slot_copy(t, 2, sib, h).start()
+
     for load in loads[: 3 * n]:
         load.wait()
-
-    @pl.when(s != t)
-    def _():
-        swapped.wait_recv()
-
-    @pl.when(s == t)
-    def _():
-        xg[t] = xb[...]
-
-    def slot_copy(slot, send, to_t):
-        return remote(xg.at[slot], xg.at[slot], send, x_recv.at[slot], s, to_t)
-
-    to_far = slot_copy(t, x_send.at[1], far)
-    to_sib = slot_copy(t, x_send.at[2], sib)
-    relay = slot_copy(far, x_send.at[3], sib)
-    to_far.start()
-    to_sib.start()
-
-    gain = gain_ref[:, pl.ds(pl.multiple_of(s * width, 128), width)]
+    gain_load.wait()
+    gain = gain_ref[...]
     ones = jnp.ones((8, width), jnp.bfloat16)
 
-    def p_copy(p, d, up):
+    cuts = (slice(0, 2 * ch), slice(2 * ch, 3 * ch))
+
+    def p_copy(p, d, up, q):
         target, recv = (from_low, low_recv) if up else (from_high, high_recv)
         return remote(
-            sendb.at[p, d], target.at[p, d], p_send.at[p, d], recv.at[p, d],
+            sendb.at[p, d, :, cuts[q]], target.at[p, d, :, cuts[q]], p_send.at[q, p, d], recv.at[q, p, d],
             s + 1 if up else s - 1, t,
         )
+
+    def first(p, q):
+        @pl.when(s == 0)
+        def _():
+            @pl.loop(0, n - 1)
+            def _(i):
+                d = n - 1 - i
+                sendb[p, d, :, cuts[q]] = part[p, d, :, cuts[q]].astype(jnp.bfloat16)
+                p_copy(p, d, True, q).start()
+
+        @pl.when(s == n - 1)
+        def _():
+            @pl.loop(0, n - 1)
+            def _(d):
+                sendb[p, d, :, cuts[q]] = part[p, d, :, cuts[q]].astype(jnp.bfloat16)
+                p_copy(p, d, False, q).start()
 
     def dots(p):
         features = xg[p].astype(jnp.float32)
@@ -267,100 +304,106 @@
         def _(d):
             part[p, d] = matmul(y, wv[d])
 
-        @pl.when(s == 0)
+    def chain(p, q):
+        @pl.when((s > 0) & (s < n - 1))
         def _():
             @pl.loop(0, n - 1)
             def _(i):
                 d = n - 1 - i
-                sendb[p, d] = part[p, d].astype(jnp.bfloat16)
-                p_copy(p, d, True).start()
-
-        @pl.when(s == n - 1)
-        def _():
-            @pl.loop(0, n - 1)
-            def _(d):
-                sendb[p, d] = part[p, d].astype(jnp.bfloat16)
-                p_copy(p, d, False).start()
-
-    def chain(p):
-        @pl.when((s > 0) & (s < n - 1))
-        def _():
-            @pl.loop(0, n - 1)
-            def _(i):
-                d = n - 1 - i
 
                 @pl.when(d > s)
                 def _():
-                    p_copy(p, d, True).wait_recv()
-                    sendb[p, d] = (part[p, d] + from_low[p, d].astype(jnp.float32)).astype(jnp.bfloat16)
-                    p_copy(p, d, True).start()
+                    p_copy(p, d, True, q).wait_recv()
+                    sendb[p, d, :, cuts[q]] = (
+                        part[p, d, :, cuts[q]] + from_low[p, d, :, cuts[q]].astype(jnp.float32)
+                    ).astype(jnp.bfloat16)
+                    p_copy(p, d, True, q).start()
 
                 @pl.when(i < s)
                 def _():
-                    p_copy(p, i, False).wait_recv()
-                    sendb[p, i] = (part[p, i] + from_high[p, i].astype(jnp.float32)).astype(jnp.bfloat16)
-                    p_copy(p, i, False).start()
-
+                    p_copy(p, i, False, q).wait_recv()
+                    sendb[p, i, :, cuts[q]] = (
+                        part[p, i, :, cuts[q]] + from_high[p, i, :, cuts[q]].astype(jnp.float32)
+                    ).astype(jnp.bfloat16)
+                    p_copy(p, i, False, q).start()
+
+    def total(p, q):
+        @pl.when(s > 0)
+        def _():
+            p_copy(p, s, True, q).wait_recv()
+            part[p, s, :, cuts[q]] += from_low[p, s, :, cuts[q]].astype(jnp.float32)
+
+        @pl.when(s < n - 1)
+        def _():
+            p_copy(p, s, False, q).wait_recv()
+            part[p, s, :, cuts[q]] += from_high[p, s, :, cuts[q]].astype(jnp.float32)
+
+    order = (t, sib, far, far_sib)
     dots(t)
-    slot_copy(sib, x_send.at[2], sib).wait_recv()
+    first(t, 0)
+    for h in range(chunks):
+        slot_copy(far, 1, far, h).wait_recv()
+        slot_copy(far, 3, sib, h).start()
+    for h in range(chunks):
+        slot_copy(sib, 2, sib, h).wait_recv()
     dots(sib)
-    slot_copy(far, x_send.at[1], far).wait_recv()
-    relay.start()
+    first(sib, 0)
     dots(far)
-    chain(t)
-    slot_copy(far_sib, x_send.at[3], sib).wait_recv()
+    first(far, 0)
+    chain(t, 0)
+    for h in range(chunks):
+        slot_copy(far_sib, 3, sib, h).wait_recv()
     dots(far_sib)
+    first(far_sib, 0)
 
     q_copies = []
     for k in range(1, n):
         q_copy = remote(squares.at[s], squares.at[s], q_send.at[k], q_recv.at[s], lax.rem(s + k, n), t)
         q_copy.start()
         q_copies.append(q_copy)
-    chain(sib)
-    chain(far)
-    chain(far_sib)
+    for p in order:
+        first(p, 1)
+    for p in order[1:]:
+        chain(p, 0)
 
     for k in range(1, n):
         other = lax.rem(s + k, n)
         remote(squares.at[other], squares.at[other], q_send.at[k], q_recv.at[other], other, t).wait_recv()
-    total = squares[0] + squares[1] + squares[2] + squares[3]
-    scale = lax.rsqrt(total * (1.0 / (n * width)) + EPSILON)
+    all_squares = squares[0] + squares[1] + squares[2] + squares[3]
+    scale = lax.rsqrt(all_squares * (1.0 / (n * width)) + EPSILON)
     scale = jnp.transpose(jnp.broadcast_to(scale[0:1], (ch, length)))
-
-    for p in (t, sib, far, far_sib):
-        @pl.when(s > 0)
-        def _():
-            p_copy(p, s, True).wait_recv()
-            part[p, s] += from_low[p, s].astype(jnp.float32)
-
-        @pl.when(s < n - 1)
-        def _():
-            p_copy(p, s, False).wait_recv()
-            part[p, s] += from_high[p, s].astype(jnp.float32)
+    taps_load.wait()
+    for p in order:
+        total(p, 0)
 
     row = lax.broadcasted_iota(jnp.int32, (length, ch), 0)
-    mixed = []
-    for j in range(3):
-        projected = jnp.concatenate([part[p, s, :, j * ch:(j + 1) * ch] for p in range(n)], axis=0) * scale
-        taps = [taps_ref[j, o:o + 1, pl.ds(pl.multiple_of(s * ch, 128), ch)] for o in range(3)]
+
+    def filtered(j):
+        at = (j + 2) % 3 * ch
+        projected = jnp.concatenate([part[p, s, :, at:at + ch] for p in range(n)], axis=0) * scale
+        taps = [taps_ref[j, o:o + 1, :] for o in range(3)]
         value = taps[0] * projected
         for o in range(1, 3):
             value = value + taps[o] * jnp.where(row >= o, pltpu.roll(projected, o, 0), 0.0)
-        mixed.append(value)
-    query = mixed[0]
-    kh, kl = two_parts(mixed[1] * mixed[2])
+        return value
+
+    kh, kl = two_parts(filtered(1) * filtered(2))
+    chain(order[0], 1)
     both = matmul(ah[...], jnp.concatenate([kh, kl], axis=1))
     signal = both[:, :ch] + both[:, ch:] + matmul(al[...], kh)
+    chain(order[1], 1)
     a, b = signal[:length], signal[length:]
     c, e = spectrum[:length], spectrum[length:]
     yh, yl = two_parts(jnp.concatenate([a * c - b * e, a * e + b * c], axis=0))
-    for load in loads[3 * n + 2:]:
+    for load in loads[3 * n + 2:3 * n + 5]:
         load.wait()
+    chain(order[2], 1)
     both = matmul(bh[...], jnp.concatenate([yh, yl], axis=1))
     conv = (both[:, :ch] + both[:, ch:] + matmul(bl[...], yh)) * (1.0 / length)
-
-    def lanes(i):
-        return pl.ds(pl.multiple_of(i * ch, 128), ch)
+    chain(order[3], 1)
+    for p in order:
+        total(p, 1)
+    query = filtered(0)
 
     gathered[:, lanes(s)] = (query * conv).astype(jnp.bfloat16)
 
@@ -399,52 +442,81 @@
     def term(p):
         return matmul_nt(gathered[pl.ds(pl.multiple_of(p * rows, 128), rows), :], wo[...])
 
-    far_out = remote(terms.at[0], sibling_in.at[0], t_send.at[0], t_recv.at[0], s, sib)
-    own_out = remote(terms.at[1], sibling_in.at[1], t_send.at[1], t_recv.at[1], s, sib)
-    cross = remote(terms.at[2], cross_in, t_send.at[2], t_recv.at[2], s, far)
-    final = remote(terms.at[3], final_in, t_send.at[3], t_recv.at[3], t, s)
+    def hop(which, target, to_s, to_t, h):
+        return remote(
+            terms.at[which, piece(h)], target.at[piece(h)], t_send.at[which, h], t_recv.at[which, h], to_s, to_t
+        )
+
+    def far_out(h):
+        return hop(0, sibling_in.at[0], s, sib, h)
+
+    def own_out(h):
+        return hop(1, sibling_in.at[1], s, sib, h)
+
+    def cross(h):
+        return hop(2, cross_in, s, far, h)
+
+    def final(h):
+        return hop(3, final_in, t, s, h)
+
     terms[0] = term(far_sib).astype(jnp.bfloat16)
-    far_out.start()
+    for h in range(chunks):
+        far_out(h).start()
+    terms_acc[...] = term(far)
+    for h in range(chunks):
+        far_out(h).wait_recv()
+        terms[2, piece(h)] = (
+            terms_acc[piece(h)] + sibling_in[0, piece(h)].astype(jnp.float32)
+        ).astype(jnp.bfloat16)
+        cross(h).start()
     terms[1] = term(sib).astype(jnp.bfloat16)
-    own_out.start()
-    far_term = term(far)
-    far_out.wait_recv()
-    terms[2] = (far_term + sibling_in[0].astype(jnp.float32)).astype(jnp.bfloat16)
-    cross.start()
-    own_term = term(t)
-    own_out.wait_recv()
-    own_term = own_term + sibling_in[1].astype(jnp.float32)
-    cross.wait_recv()
-    own_term = own_term + cross_in[...].astype(jnp.float32)
+    for h in range(chunks):
+        own_out(h).start()
+    terms_acc[...] = term(t)
+    for h in range(chunks):
+        own_out(h).wait_recv()
+        terms_acc[piece(h)] += sibling_in[1, piece(h)].astype(jnp.float32)
+    for h in range(chunks):
+        cross(h).wait_recv()
+        value = terms_acc[piece(h)] + cross_in[piece(h)].astype(jnp.float32)
+
+        @pl.when(s != t)
+        def _():
+            terms[3, piece(h)] = value.astype(jnp.bfloat16)
+            final(h).start()
+
+        @pl.when(s == t)
+        def _():
+            out_ref[piece(h)] = x_ref[piece(h)] + value
 
     @pl.when(s != t)
     def _():
-        terms[3] = own_term.astype(jnp.bfloat16)
-        final.start()
-        final.wait_recv()
-        out_ref[...] = x_ref[...] + final_in[...].astype(jnp.float32)
-
-    @pl.when(s == t)
-    def _():
-        out_ref[...] = x_ref[...] + own_term
-
-    @pl.when(s != t)
-    def _():
-        swap.wait_send()
-        final.wait_send()
-
-    for copy in [to_far, to_sib, relay, far_out, own_out, cross] + q_copies:
+        for h in range(chunks):
+            final(h).wait_recv()
+            out_ref[piece(h)] = x_ref[piece(h)] + final_in[piece(h)].astype(jnp.float32)
+        for h in range(chunks):
+            swap(h, s).wait_send()
+            final(h).wait_send()
+
+    for h in range(chunks):
+        for copy in (
+            slot_copy(t, 1, far, h), slot_copy(t, 2, sib, h), slot_copy(far, 3, sib, h),
+            far_out(h), own_out(h), cross(h),
+        ):
+            copy.wait_send()
+    for copy in q_copies:
         copy.wait_send()
-    for p in (t, sib, far, far_sib):
-        @pl.loop(0, n)
-        def _(d):
-            @pl.when(d > s)
-            def _():
-                p_copy(p, d, True).wait_send()
-
-            @pl.when(d < s)
-            def _():
-                p_copy(p, d, False).wait_send()
+    for p in order:
+        for q in range(2):
+            @pl.loop(0, n)
+            def _(d):
+                @pl.when(d > s)
+                def _():
+                    p_copy(p, d, True, q).wait_send()
+
+                @pl.when(d < s)
+                def _():
+                    p_copy(p, d, False, q).wait_send()
 
     @pl.loop(0, n)
     def _(i):
@@ -468,9 +540,13 @@
     return pl.pallas_call(
         block_kernel,
         out_shape=jax.ShapeDtypeStruct((rows, width), f32),
-        in_specs=[vmem, vmem, hbm, vmem, vmem] + [hbm] * 5,
+        in_specs=[hbm] * 10,
         out_specs=vmem,
         scratch_shapes=[
+            pltpu.VMEM((rows, width), f32),
+            pltpu.VMEM((1, width), f32),
+            pltpu.VMEM(short_taps.shape[:2] + (ch,), f32),
+            pltpu.VMEM((ch, length), f32),
             pltpu.VMEM((n, width, 3 * ch), bf16),
             pltpu.VMEM(out_weight.shape, bf16),
             pltpu.VMEM((2 * length, length), bf16),
@@ -487,14 +563,15 @@
             pltpu.VMEM((2 * length, ch), f32),
             pltpu.VMEM((length, n * ch), bf16),
             pltpu.VMEM((n, rows, width), bf16),
+            pltpu.VMEM((rows, width), f32),
             pltpu.VMEM((2, rows, width), bf16),
             pltpu.VMEM((rows, width), bf16),
             pltpu.VMEM((rows, width), bf16),
-            dma((3 * n + 5,)), dma((n,)), dma((n,)), dma((n, n)), dma((n, n)), dma((n, n)),
-            dma((n,)), dma((n,)), dma((n,)), dma((n,)), dma((n,)), dma((n,)), dma((n,)),
+            dma((3 * n + 9,)), dma((n, n)), dma((n, n)), dma((2, n, n)), dma((2, n, n)), dma((2, n, n)),
+            dma((n,)), dma((n,)), dma((n,)), dma((n,)), dma((n,)), dma((n, n)), dma((n, n)),
         ],
         compiler_params=pltpu.CompilerParams(
-            collective_id=0, has_side_effects=True, vmem_limit_bytes=48 * 1024 * 1024
+            collective_id=0, has_side_effects=True, vmem_limit_bytes=60 * 1024 * 1024
         ),
     )(residual_in, norm_gain[None], in_weight, short_taps, long_filter, out_weight, *tables)
 

time: 109 us -> 119 us (1.092)
  the two profiles are of different devices: /device:TPU:16 before, /device:TPU:3 now
where the time goes in v2:
time: 119 us; the launch traced here: 118 us
  Pallas kernels  117 us (98%)
  local copies, waits for them, and re-layouts  1.89 us (2%)
    pallas_call x1, Pallas kernels, kernel_shards(): pl.pallas_call(block_kernel, out_shape=jax.ShapeDtypeStruct((rows, width)...  117 us

profile of v2, /device:TPU:3, one launch (start us, length us, event | category | flops | bytes accessed | tf_op | source)
XLA Modules:
  0.0 118.4 jit_solution(12032313861178970704)
XLA Ops:
  0.0 116.5 %shard_map.100 = f32[128,1024]{1,0:T(8,128)} custom-call(f32[128,1024]{1,0:T(8,128)} %x_hbm.1, f32[1,4096]{1,0:T(1,128)} %bitcast.1, bf16[3,1024,512]{2,1,0:T(8,128)(2,1)} %w_hbm.1, f32[3,3,512]{2,1,0:T(4,128)} %taps_hbm.1, f32[128,512]{1,0:T(8,128)} %filter_hbm.1, bf16[1024,512]{1,0:T(8,128)(2,1)} %wo_hbm.1, bf16[1024,512]{1,0:T(8,128)(2,1)} %constant.8.clone.ah_hbm, ...), custom_call_target="tpu_custom_call" | custom-call | tf_op jit(solution)/shard_map/pallas_call | solution.py:540
  116.5 1.9 %copy.12 = f32[128,1024]{1,0:T(8,128)} copy(f32[128,1024]{1,0:T(8,128)} %shard_map.100) | data formatting | bytes 1048576
